TPU v7x, 32 devices: a whole 2x2x4 slice. The times are simulated.
32 devices in a mesh: store: 8 (over y, x, core), tp: 4 (over z).
Axes of the slice: x: 2, y: 2, z: 4, core: 2. Of those that a mesh axis runs over, the one named last changes fastest.
Arguments:
- queries: bfloat16 [8, 512, 4096], P('store', 'tp')
- suffix_keys: bfloat16 [8, 512, 512], P('store', 'tp'), may hold values from -6 to 6
- suffix_values: bfloat16 [8, 512, 512], P('store', 'tp'), may hold values from -6 to 6
- passage_keys: bfloat16 [8, 2048, 512], P(None, 'store')
- passage_values: bfloat16 [8, 2048, 512], P(None, 'store'), may hold values from -6 to 6
- cites: int32 [8, 2], replicated, may hold values from 0 to 7, all different within a row
- passage_row: int32 [8], replicated, may hold values from 0 to 7, each once
- suffix_len: int32 [8], replicated, may hold values from 1 to 512, as said below
Outputs:
- context: bfloat16 [8, 512, 4096], P('store', 'tp')
- decode_keys: bfloat16 [8, 512, 512], P('store', None, 'tp')
- decode_values: bfloat16 [8, 512, 512], P('store', None, 'tp')
Inputs may be any that keep to these rules, and one draw needn't show every extreme that they name: Each request cites 2 different passages; every passage is cited by some request. `passage_row`: each store row holds exactly one passage id. `suffix_len`: some request has all 512 suffix tokens live.
All inputs are finite; a program needn't handle non-finite values.
Results may differ from a plain program's by a relative error of at most 0.0085.
Values may be sent and summed in bfloat16 or wider, within the bound.
A program may use at most 128 MiB of HBM per device.

v0:
```python
import jax
import jax.numpy as jnp
from jax import lax
from jax.sharding import PartitionSpec as P

HD = 128


def attend(query_rows, keys, values, positions, length, prefix):
    rows = query_rows.shape[0]
    kv_count = keys.shape[1] // HD
    groups = query_rows.shape[1] // (kv_count * HD)
    total = keys.shape[0]
    key_index = jnp.arange(total, dtype=jnp.int32)
    visible = (key_index[None, :] < prefix) | (key_index[None, :] - prefix <= positions[:, None])
    query_heads = query_rows.reshape(rows, kv_count, groups, HD).transpose(1, 0, 2, 3)
    key_heads = keys.reshape(total, kv_count, HD).transpose(1, 0, 2)
    value_heads = values.reshape(total, kv_count, HD).transpose(1, 0, 2)
    scale = HD ** (-0.5)

    def one_head(item):
        query_g, key_g, value_g = item
        scores = (
            jnp.einsum("rgd,kd->rgk", query_g, key_g, preferred_element_type=jnp.float32) * scale
        )
        scores = jnp.where(visible[:, None, :], scores, -1e30)
        peak = jnp.max(scores, axis=-1, keepdims=True)
        weights = jnp.exp(scores - peak)
        probs = (weights / jnp.sum(weights, axis=-1, keepdims=True)).astype(jnp.bfloat16)
        return jnp.einsum("rgk,kd->rgd", probs, value_g, preferred_element_type=jnp.float32)

    output = lax.map(one_head, (query_heads, key_heads, value_heads))
    output = output.transpose(1, 0, 2, 3).reshape(rows, kv_count * groups * HD)
    live = (positions < length)[:, None]
    return (output * live).astype(jnp.bfloat16)


def body(
    queries,
    suffix_keys,
    suffix_values,
    passage_keys,
    passage_values,
    cites,
    passage_row,
    suffix_len,
):
    n_tp = lax.axis_size("tp")
    request = lax.axis_index("store")
    rank = lax.axis_index("tp")
    tok_rows = queries.shape[1]
    suffix_total = tok_rows * n_tp
    width = suffix_keys.shape[2]
    length = suffix_len[request]
    wanted = passage_row[cites]
    prefix = cites.shape[1] * passage_keys.shape[1] * lax.axis_size("store")
    send_keys = passage_keys[wanted]
    send_values = passage_values[wanted]
    got_keys, got_values = (
        lax.all_to_all(send_keys, "store", split_axis=0, concat_axis=0, tiled=True),
        lax.all_to_all(send_values, "store", split_axis=0, concat_axis=0, tiled=True),
    )
    whole_keys, whole_values = (
        lax.all_gather(suffix_keys[0], "tp", axis=0, tiled=True),
        lax.all_gather(suffix_values[0], "tp", axis=0, tiled=True),
    )
    keys = jnp.concatenate([got_keys.reshape(-1, width), whole_keys], axis=0)
    values = jnp.concatenate([got_values.reshape(-1, width), whole_values], axis=0)
    positions = rank * tok_rows + jnp.arange(tok_rows, dtype=jnp.int32)
    context = attend(queries[0], keys, values, positions, length, prefix)[None]
    slice_width = width // n_tp
    own_keys = lax.dynamic_slice_in_dim(whole_keys, rank * slice_width, slice_width, 1)
    own_values = lax.dynamic_slice_in_dim(whole_values, rank * slice_width, slice_width, 1)
    live = (jnp.arange(suffix_total, dtype=jnp.int32) < length)[:, None]
    decode_keys = jnp.where(live, own_keys, jnp.zeros_like(own_keys))[None]
    decode_values = jnp.where(live, own_values, jnp.zeros_like(own_values))[None]
    return (context, decode_keys, decode_values)


def solution(mesh):
    in_specs = (
        P("store", "tp", None),
        P("store", "tp", None),
        P("store", "tp", None),
        P(None, "store", None),
        P(None, "store", None),
        P(),
        P(),
        P(),
    )
    out_specs = (P("store", "tp", None), P("store", None, "tp"), P("store", None, "tp"))
    return jax.shard_map(body, mesh=mesh, in_specs=in_specs, out_specs=out_specs, check_vma=False)
```

profile of v0, /device:TPU:0, one launch (start us, length us, event | category | flops | bytes accessed | tf_op | source)
XLA Modules:
  0.0 282.0 jit_solution(15693270275199861389)
XLA Ops:
  1.7 1.3 gather_fusion
  3.2 2.8 gather_fusion.1
  5.9 5.3 %all-to-all-start = ((bf16[8,2,256,512]{3,2,1,0:T(8,128)(2,1)}), bf16[8,2,256,512]{3,2,1,0:T(8,128)(2,1)}, u32[]{:S(2)}, u32[]{:S(2)}) async-start(bf16[8,2,256,512]{3,2,1,0:T(8,128)(2,1)} %bitcast.58), calls=%async_computation | async-start | bytes 8388608 | tf_op jit(solution)/shard_map/all_to_all | solution.py:60
  11.2 2.8 gather_fusion.2
  14.0 46.4 %all-to-all-done = bf16[8,2,256,512]{3,2,1,0:T(8,128)(2,1)} async-done(((bf16[8,2,256,512]{3,2,1,0:T(8,128)(2,1)}), bf16[8,2,256,512]{3,2,1,0:T(8,128)(2,1)}, u32[]{:S(2)}, u32[]{:S(2)}) %all-to-all-start) | async-done | bytes 4194336 | tf_op jit(solution)/shard_map/all_to_all | solution.py:60
  60.4 4.7 %all-to-all-start.1 = ((bf16[8,2,256,512]{3,2,1,0:T(8,128)(2,1)}), bf16[8,2,256,512]{3,2,1,0:T(8,128)(2,1)}, u32[]{:S(2)}, u32[]{:S(2)}) async-start(bf16[8,2,256,512]{3,2,1,0:T(8,128)(2,1)} %bitcast.57), calls=%async_computation.1 | async-start | bytes 8388608 | tf_op jit(solution)/shard_map/all_to_all | solution.py:61
  65.3 16.4 %all-gather = bf16[1,512,512]{1,2,0:T(8,128)(2,1)S(1)} all-gather(bf16[1,128,512]{1,2,0:T(8,128)(2,1)S(1)} %copy.25), channel_id=2, replica_groups=mesh['store'=8,'tp'=4] {'tp'}, dimensions={1}, use_global_device_ids=true | all-gather | bytes 655360 | tf_op jit(solution)/shard_map/all_gather | solution.py:64
  82.0 14.9 %all-gather.1 = bf16[1,512,512]{1,2,0:T(8,128)(2,1)S(1)} all-gather(bf16[1,128,512]{1,2,0:T(8,128)(2,1)S(1)} %copy.27), channel_id=3, replica_groups=mesh['store'=8,'tp'=4] {'tp'}, dimensions={1}, use_global_device_ids=true | all-gather | bytes 655360 | tf_op jit(solution)/shard_map/all_gather | solution.py:65
  97.7 1.6 copy.23
  100.6 1.2 compare_convert_fusion
  102.6 6.9 %concatenate.16 = bf16[4096,4,128]{2,1,0:T(4,128)(2,1)} reshape(bf16[8,2,256,512]{3,2,1,0:T(8,128)(2,1)} %all-to-all-done) | data formatting | bytes 8388608 | tf_op jit(solution)/shard_map/concatenate | solution.py:67
  109.5 19.2 %maximum_bitcast_fusion = bf16[4,4608,128]{2,0,1:T(4,128)(2,1)S(1)} fusion(bf16[512,4,128]{2,1,0:T(4,128)(2,1)S(1)} %copy.26, bf16[4096,4,128]{2,1,0:T(4,128)(2,1)} %concatenate.16), kind=kLoop, calls=%fused_computation.27 | loop fusion | flops 2359296 | bytes 9437184 | tf_op jit(solution)/shard_map/transpose | solution.py:17
  128.7 2.8 copy.30
  131.5 7.0 %concatenate.19 = bf16[4096,4,128]{2,1,0:T(4,128)(2,1)} reshape(bf16[8,2,256,512]{3,2,1,0:T(8,128)(2,1)} %all-to-all-done.1) | data formatting | bytes 8388608 | tf_op jit(solution)/shard_map/concatenate | solution.py:68
  138.5 19.2 %maximum_bitcast_fusion.1 = bf16[4,4608,128]{2,0,1:T(4,128)(2,1)S(1)} fusion(bf16[512,4,128]{2,1,0:T(4,128)(2,1)S(1)} %copy.28, bf16[4096,4,128]{2,1,0:T(4,128)(2,1)} %concatenate.19), kind=kLoop, calls=%fused_computation.28 | loop fusion | flops 2359296 | bytes 9437184 | tf_op jit(solution)/shard_map/transpose | solution.py:18
  157.7 2.8 %copy.31 = bf16[4,4608,128]{2,1,0:T(8,128)(2,1)} copy(bf16[4,4608,128]{2,0,1:T(4,128)(2,1)S(1)} %maximum_bitcast_fusion.1) | data formatting | bytes 9437184
  160.5 111.7 %while.11 = (s32[]{:T(128)}, f32[4,128,8,128]{3,1,2,0:T(8,128)}, bf16[4,128,8,128]{1,3,2,0:T(8,128)(2,1)S(1)}, bf16[4,4608,128]{2,1,0:T(8,128)(2,1)}, bf16[4,460...) while((s32[]{:T(128)}, f32[4,128,8,128]{3,1,2,0:T(8,128)}, ...), condition=%wide.region_3.4_spmd.clone, body=%wide.region_0.3_spmd.clone.sunk | while | flops 2454852096 | bytes 79856736 | solution.py:32
  160.5 3.9 %fusion.33 = f32[128,8,4608]{2,0,1:T(8,128)S(1)} fusion(bf16[4,4608,128]{2,1,0:T(8,128)(2,1)} %get-tuple-element.167, s32[]{:T(128)} %get-tuple-element.155, bf16[4,128,8,128]{1,3,2,0:T(8,128)(2,1)S(1)} %get-tuple-element.166), kind=kOutput, calls=%fused_computation.17.clone.1 | convolution fusion | flops 1207959552 | bytes 20317184 | tf_op jit(solution)/shard_map/while/body/eval_jaxpr/rgd,kd->rgk/dot_general | solution.py:24
  164.9 13.4 %fusion.34 = (f32[128,8]{0,1:T(8,128)S(1)}, f32[128,8,4608]{2,0,1:T(8,128)}) fusion(f32[128,8,4608]{2,0,1:T(8,128)S(1)} %fusion.33, pred[128,4608]{1,0:T(8,128)(4,1)S(1)} %compare_or_fusion.2), kind=kOutput, calls=%fused_computation.45.clone.1 | output fusion | flops 28316160 | bytes 38342656 | tf_op jit(solution)/shard_map/while/body/eval_jaxpr/sub | solution.py:28
  178.3 10.1 %fusion.35 = f32[4,128,8,128]{3,1,2,0:T(8,128)} fusion(f32[4,128,8,128]{3,1,2,0:T(8,128)} %get-tuple-element.156, s32[]{:T(128)} %get-tuple-element.155, f32[128,8,4608]{2,0,1:T(8,128)} %get-tuple-element.144, f32[128,8]{0,1:T(8,128)S(1)} %get-tuple-element.145, bf16[4,4608,128]{2,1,0:T(8,128)(2,1)} %get-tuple-element.168), kind=kOutput, calls=%fused_computation.15.clone.1 | convolution fusion | flops 1217396736 | bytes 20583424 | tf_op jit(solution)/shard_map/while/body/eval_jaxpr/rgk,kd->rgd/dot_general | solution.py:30
  188.4 3.9 %fusion.33 = f32[128,8,4608]{2,0,1:T(8,128)S(1)} fusion(bf16[4,4608,128]{2,1,0:T(8,128)(2,1)} %get-tuple-element.167, s32[]{:T(128)} %get-tuple-element.155, bf16[4,128,8,128]{1,3,2,0:T(8,128)(2,1)S(1)} %get-tuple-element.166), kind=kOutput, calls=%fused_computation.17.clone.1 | convolution fusion | flops 1207959552 | bytes 20317184 | tf_op jit(solution)/shard_map/while/body/eval_jaxpr/rgd,kd->rgk/dot_general | solution.py:24
  192.8 13.4 %fusion.34 = (f32[128,8]{0,1:T(8,128)S(1)}, f32[128,8,4608]{2,0,1:T(8,128)}) fusion(f32[128,8,4608]{2,0,1:T(8,128)S(1)} %fusion.33, pred[128,4608]{1,0:T(8,128)(4,1)S(1)} %compare_or_fusion.2), kind=kOutput, calls=%fused_computation.45.clone.1 | output fusion | flops 28316160 | bytes 38342656 | tf_op jit(solution)/shard_map/while/body/eval_jaxpr/sub | solution.py:28
  206.2 10.1 %fusion.35 = f32[4,128,8,128]{3,1,2,0:T(8,128)} fusion(f32[4,128,8,128]{3,1,2,0:T(8,128)} %get-tuple-element.156, s32[]{:T(128)} %get-tuple-element.155, f32[128,8,4608]{2,0,1:T(8,128)} %get-tuple-element.144, f32[128,8]{0,1:T(8,128)S(1)} %get-tuple-element.145, bf16[4,4608,128]{2,1,0:T(8,128)(2,1)} %get-tuple-element.168), kind=kOutput, calls=%fused_computation.15.clone.1 | convolution fusion | flops 1217396736 | bytes 20583424 | tf_op jit(solution)/shard_map/while/body/eval_jaxpr/rgk,kd->rgd/dot_general | solution.py:30
  216.3 3.9 %fusion.33 = f32[128,8,4608]{2,0,1:T(8,128)S(1)} fusion(bf16[4,4608,128]{2,1,0:T(8,128)(2,1)} %get-tuple-element.167, s32[]{:T(128)} %get-tuple-element.155, bf16[4,128,8,128]{1,3,2,0:T(8,128)(2,1)S(1)} %get-tuple-element.166), kind=kOutput, calls=%fused_computation.17.clone.1 | convolution fusion | flops 1207959552 | bytes 20317184 | tf_op jit(solution)/shard_map/while/body/eval_jaxpr/rgd,kd->rgk/dot_general | solution.py:24
  220.7 13.4 %fusion.34 = (f32[128,8]{0,1:T(8,128)S(1)}, f32[128,8,4608]{2,0,1:T(8,128)}) fusion(f32[128,8,4608]{2,0,1:T(8,128)S(1)} %fusion.33, pred[128,4608]{1,0:T(8,128)(4,1)S(1)} %compare_or_fusion.2), kind=kOutput, calls=%fused_computation.45.clone.1 | output fusion | flops 28316160 | bytes 38342656 | tf_op jit(solution)/shard_map/while/body/eval_jaxpr/sub | solution.py:28
  234.2 10.1 %fusion.35 = f32[4,128,8,128]{3,1,2,0:T(8,128)} fusion(f32[4,128,8,128]{3,1,2,0:T(8,128)} %get-tuple-element.156, s32[]{:T(128)} %get-tuple-element.155, f32[128,8,4608]{2,0,1:T(8,128)} %get-tuple-element.144, f32[128,8]{0,1:T(8,128)S(1)} %get-tuple-element.145, bf16[4,4608,128]{2,1,0:T(8,128)(2,1)} %get-tuple-element.168), kind=kOutput, calls=%fused_computation.15.clone.1 | convolution fusion | flops 1217396736 | bytes 20583424 | tf_op jit(solution)/shard_map/while/body/eval_jaxpr/rgk,kd->rgd/dot_general | solution.py:30
  244.3 3.9 %fusion.33 = f32[128,8,4608]{2,0,1:T(8,128)S(1)} fusion(bf16[4,4608,128]{2,1,0:T(8,128)(2,1)} %get-tuple-element.167, s32[]{:T(128)} %get-tuple-element.155, bf16[4,128,8,128]{1,3,2,0:T(8,128)(2,1)S(1)} %get-tuple-element.166), kind=kOutput, calls=%fused_computation.17.clone.1 | convolution fusion | flops 1207959552 | bytes 20317184 | tf_op jit(solution)/shard_map/while/body/eval_jaxpr/rgd,kd->rgk/dot_general | solution.py:24
  248.7 13.4 %fusion.34 = (f32[128,8]{0,1:T(8,128)S(1)}, f32[128,8,4608]{2,0,1:T(8,128)}) fusion(f32[128,8,4608]{2,0,1:T(8,128)S(1)} %fusion.33, pred[128,4608]{1,0:T(8,128)(4,1)S(1)} %compare_or_fusion.2), kind=kOutput, calls=%fused_computation.45.clone.1 | output fusion | flops 28316160 | bytes 38342656 | tf_op jit(solution)/shard_map/while/body/eval_jaxpr/sub | solution.py:28
  262.1 10.1 %fusion.35 = f32[4,128,8,128]{3,1,2,0:T(8,128)} fusion(f32[4,128,8,128]{3,1,2,0:T(8,128)} %get-tuple-element.156, s32[]{:T(128)} %get-tuple-element.155, f32[128,8,4608]{2,0,1:T(8,128)} %get-tuple-element.144, f32[128,8]{0,1:T(8,128)S(1)} %get-tuple-element.145, bf16[4,4608,128]{2,1,0:T(8,128)(2,1)} %get-tuple-element.168), kind=kOutput, calls=%fused_computation.15.clone.1 | convolution fusion | flops 1217396736 | bytes 20583424 | tf_op jit(solution)/shard_map/while/body/eval_jaxpr/rgk,kd->rgd/dot_general | solution.py:30
  272.2 4.3 %copy.32 = f32[128,4,8,128]{3,2,1,0:T(8,128)} copy(f32[128,4,8,128]{3,0,2,1:T(8,128)} %bitcast.62) | data formatting | bytes 4194304 | tf_op jit(solution)/shard_map/transpose | solution.py:33
  276.5 2.7 reshape.90
  279.2 2.8 multiply_convert_fusion
  (42 shorter events, 6.3 us)
Async XLA Ops:
  0.6 2.5 copy-start
  5.9 5.3 %copy-start.2 = (bf16[8,256,512]{2,1,0:T(8,128)(2,1)S(1)}, bf16[8,256,512]{2,1,0:T(8,128)(2,1)}, u32[]{:S(2)}) copy-start(bf16[8,256,512]{2,1,0:T(8,128)(2,1)} %param.14) | copy-start | bytes 6291460
  5.9 54.5 %all-to-all-start = ((bf16[8,2,256,512]{3,2,1,0:T(8,128)(2,1)}), bf16[8,2,256,512]{3,2,1,0:T(8,128)(2,1)}, u32[]{:S(2)}, u32[]{:S(2)}) async-start(bf16[8,2,256,512]{3,2,1,0:T(8,128)(2,1)} %bitcast.58), calls=%async_computation | async-start | bytes 8388608 | tf_op jit(solution)/shard_map/all_to_all | solution.py:60
  14.0 51.2 %copy-start.3 = (bf16[1,128,512]{2,1,0:T(8,128)(2,1)S(1)}, bf16[1,128,512]{2,1,0:T(8,128)(2,1)}, u32[]{:S(2)}) copy-start(bf16[1,128,512]{2,1,0:T(8,128)(2,1)} %param.11) | copy-start | bytes 393220
  60.4 21.4 %copy-start.4 = (bf16[1,128,512]{2,1,0:T(8,128)(2,1)S(1)}, bf16[1,128,512]{2,1,0:T(8,128)(2,1)}, u32[]{:S(2)}) copy-start(bf16[1,128,512]{2,1,0:T(8,128)(2,1)} %param.12) | copy-start | bytes 393220
  60.4 71.1 %all-to-all-start.1 = ((bf16[8,2,256,512]{3,2,1,0:T(8,128)(2,1)}), bf16[8,2,256,512]{3,2,1,0:T(8,128)(2,1)}, u32[]{:S(2)}, u32[]{:S(2)}) async-start(bf16[8,2,256,512]{3,2,1,0:T(8,128)(2,1)} %bitcast.57), calls=%async_computation.1 | async-start | bytes 8388608 | tf_op jit(solution)/shard_map/all_to_all | solution.py:61
  65.1 34.2 %copy-start.6 = (s32[8]{0:T(128)S(1)}, s32[8]{0:T(128)}, u32[]{:S(2)}) copy-start(s32[8]{0:T(128)} %param.17) | copy-start | bytes 100
  272.2 7.0 %copy-start.5 = (f32[128]{0:T(128)S(1)}, f32[128]{0:T(128)}, u32[]{:S(2)}) copy-start(f32[128]{0:T(128)} %compare_convert_fusion) | copy-start | bytes 1540
  272.2 9.8 %copy-start.1 = (bf16[8,256,512]{2,1,0:T(8,128)(2,1)S(1)}, bf16[8,256,512]{2,1,0:T(8,128)(2,1)}, u32[]{:S(2)}) copy-start(bf16[8,256,512]{2,1,0:T(8,128)(2,1)} %param.13) | copy-start | bytes 6291460
where the time goes:
time: 283 us; the launch traced here: 282 us
  other arithmetic  100 us (35%)
  matrix products  56.1 us (20%)
  waiting for transfers between devices  46.4 us (16%)
  local copies, waits for them, and re-layouts  37.1 us (13%)
  blocking collectives  31.3 us (11%)
  starting transfers between devices  9.99 us (4%)
    sub x4, other arithmetic, one_head(): weights = jnp.exp(scores - peak)  53.7 us
    all_to_all x1, waiting for transfers between devices, body(): lax.all_to_all(send_keys, 'store', split_axis=0, concat_axis=0, tiled=True)  46.4 us
    dot_general x4, matrix products, one_head(): jnp.einsum('rgk,kd->rgd', probs, value_g, preferred_element_type=jnp.floa...  40.4 us
    transpose x1, other arithmetic, attend(): key_heads = keys.reshape(total, kv_count, HD).transpose(1, 0, 2)  19.2 us
    transpose x1, other arithmetic, attend(): value_heads = values.reshape(total, kv_count, HD).transpose(1, 0, 2)  19.2 us
    all_gather x1, blocking collectives, body(): lax.all_gather(suffix_keys[0], 'tp', axis=0, tiled=True)  16.4 us
    dot_general x4, matrix products, one_head(): jnp.einsum('rgd,kd->rgk', query_g, key_g, preferred_element_type=jnp.floa...  15.7 us
    all_gather x1, blocking collectives, body(): lax.all_gather(suffix_values[0], 'tp', axis=0, tiled=True)  14.9 us
  transfers between devices with their start and end apart: 2, of which 1 were waited for; matrix products, arithmetic and copies ran while one was open for 13% of the time, Pallas kernels for 0%

commit v1 on v0

v1 whole, which is shorter than its diff:
```python
import functools
import math

import jax
import jax.numpy as jnp
from jax import lax
from jax.experimental import pallas as pl
from jax.experimental.pallas import tpu as pltpu
from jax.sharding import PartitionSpec as P

HD = 128
STEP_KEYS = 1024
STACK = 4
FACTOR = HD ** (-0.5) * math.log2(math.e)


def flip(me, d, n):
    out, bit = 0, 1
    while bit < n:
        out = out + ((me // bit + d // bit) % 2) * bit
        bit *= 2
    return out


def pick_kernel(n, cite, rows_ref, rank_ref, pk_ref, pv_ref, out_ref, sem):
    column = pl.ds(pl.multiple_of(rank_ref[0] * HD, HD), HD)

    def copies(i):
        made = []
        for c in range(cite):
            row = rows_ref[i, c]
            for which, ref in enumerate((pk_ref, pv_ref)):
                made.append(
                    pltpu.make_async_copy(
                        ref.at[row, :, column], out_ref.at[i, which, c], sem.at[i, c, which]
                    )
                )
        return made

    @pl.loop(0, n)
    def _(i):
        for copy in copies(i):
            copy.start()

    @pl.loop(0, n)
    def _(i):
        for copy in copies(i):
            copy.wait()


def pick(rows, rank, passage_keys, passage_values):
    n, cite = rows.shape
    part = passage_keys.shape[1]
    return pl.pallas_call(
        functools.partial(pick_kernel, n, cite),
        out_shape=jax.ShapeDtypeStruct((n, 2, cite, part, HD), passage_keys.dtype),
        in_specs=[
            pl.BlockSpec(memory_space=pltpu.SMEM),
            pl.BlockSpec(memory_space=pltpu.SMEM),
            pl.BlockSpec(memory_space=pl.ANY),
            pl.BlockSpec(memory_space=pl.ANY),
        ],
        out_specs=pl.BlockSpec(memory_space=pl.ANY),
        scratch_shapes=[pltpu.SemaphoreType.DMA((n, cite, 2))],
        name="pick",
    )(rows, rank, passage_keys, passage_values)


def attend_kernel(
    n_store, n_tp, group, heads,
    q_ref, sk_ref, sv_ref, send_ref, ctx_ref, dk_ref, dv_ref,
    qbuf, kvbuf, skbuf, svbuf, obuf, acc, peak,
    kv_send, kv_recv, q_send, q_recv, s_send, s_recv, c_send, c_recv, own_sem,
):
    me = lax.axis_index("store")
    rank = lax.axis_index("tp")
    tok = q_ref.shape[0]
    width = heads * HD
    steps = n_store // group
    keys_in = kvbuf.shape[2]
    MESH = pl.DeviceIdType.MESH

    def columns(index, size):
        return pl.ds(pl.multiple_of(index * size, size), size)

    def kv_copy(d):
        return pltpu.make_async_remote_copy(
            src_ref=send_ref.at[d], dst_ref=kvbuf.at[d],
            send_sem=kv_send.at[d], recv_sem=kv_recv.at[d],
            device_id=(flip(me, d, n_store), rank), device_id_type=MESH,
        )

    def q_copy(d):
        other = flip(rank, d, n_tp)
        return pltpu.make_async_remote_copy(
            src_ref=q_ref.at[:, columns(other, width)], dst_ref=qbuf.at[d],
            send_sem=q_send.at[d], recv_sem=q_recv.at[d],
            device_id=(me, other), device_id_type=MESH,
        )

    def s_copies(d):
        other = flip(rank, d, n_tp)
        return [
            pltpu.make_async_remote_copy(
                src_ref=src.at[:, columns(other, HD)], dst_ref=dst.at[columns(rank, tok)],
                send_sem=s_send.at[w, d], recv_sem=s_recv.at[w, d],
                device_id=(me, other), device_id_type=MESH,
            )
            for w, (src, dst) in enumerate(((sk_ref, skbuf), (sv_ref, svbuf)))
        ]

    def s_arrivals(d):
        other = flip(rank, d, n_tp)
        return [
            pltpu.make_async_remote_copy(
                src_ref=src.at[:, columns(other, HD)], dst_ref=dst.at[columns(other, tok)],
                send_sem=s_send.at[w, d], recv_sem=s_recv.at[w, d],
                device_id=(me, other), device_id_type=MESH,
            )
            for w, (src, dst) in enumerate(((sk_ref, skbuf), (sv_ref, svbuf)))
        ]

    def c_copy(d):
        other = flip(rank, d, n_tp)
        return pltpu.make_async_remote_copy(
            src_ref=obuf.at[d], dst_ref=ctx_ref.at[:, columns(rank, width)],
            send_sem=c_send.at[d], recv_sem=c_recv.at[d],
            device_id=(me, other), device_id_type=MESH,
        )

    def c_arrival(d):
        other = flip(rank, d, n_tp)
        return pltpu.make_async_remote_copy(
            src_ref=obuf.at[d], dst_ref=ctx_ref.at[:, columns(other, width)],
            send_sem=c_send.at[d], recv_sem=c_recv.at[d],
            device_id=(me, other), device_id_type=MESH,
        )

    own = [
        pltpu.make_async_copy(q_ref.at[:, columns(rank, width)], qbuf.at[0], own_sem.at[0]),
        pltpu.make_async_copy(send_ref.at[0], kvbuf.at[0], own_sem.at[1]),
        pltpu.make_async_copy(sk_ref.at[:, columns(rank, HD)], skbuf.at[columns(rank, tok)], own_sem.at[2]),
        pltpu.make_async_copy(sv_ref.at[:, columns(rank, HD)], svbuf.at[columns(rank, tok)], own_sem.at[3]),
    ]
    for copy in own:
        copy.start()

    barrier = pltpu.get_barrier_semaphore()

    @pl.loop(1, n_store)
    def _(d):
        pl.semaphore_signal(barrier, inc=1, device_id=(flip(me, d, n_store), rank), device_id_type=MESH)

    for d in range(1, n_tp):
        pl.semaphore_signal(barrier, inc=1, device_id=(me, flip(rank, d, n_tp)), device_id_type=MESH)
    pl.semaphore_wait(barrier, n_store - 1 + n_tp - 1)

    for d in range(1, n_tp):
        q_copy(d).start()

    @pl.loop(1, n_store)
    def _(d):
        kv_copy(d).start()

    for d in range(1, n_tp):
        for copy in s_copies(d):
            copy.start()

    peak[...] = jnp.full_like(peak, -jnp.inf)
    acc[...] = jnp.zeros_like(acc)

    def unit(q, keys, values, hidden=None):
        count = keys.shape[0]
        wide = jnp.concatenate([values, jnp.ones_like(values)], axis=1)
        for first in range(0, heads, STACK):
            stacked = jnp.concatenate(
                [qbuf[q, :, h * HD:(h + 1) * HD] for h in range(first, first + STACK)], axis=0
            )
            scores = lax.dot_general(
                stacked, keys, (((1,), (1,)), ((), ())), preferred_element_type=jnp.float32
            )
            if hidden is not None:
                scores = jnp.where(hidden, -1e30, scores)
            rows = STACK * tok
            before = peak[q, first:first + STACK].reshape(rows, HD)
            now = jnp.maximum(before, jnp.max(scores, axis=1, keepdims=True))
            decay = jnp.exp2((before - now) * FACTOR)
            base = now * FACTOR
            weights = jnp.exp2(
                scores * FACTOR - jnp.concatenate([base] * (count // HD), axis=1)
            ).astype(jnp.bfloat16)
            part = jnp.dot(weights, wide, preferred_element_type=jnp.float32)
            held = acc[q, first:first + STACK].reshape(rows, 2 * HD)
            acc[q, first:first + STACK] = (
                held * jnp.concatenate([decay, decay], axis=1) + part
            ).reshape(STACK, tok, 2 * HD)
            peak[q, first:first + STACK] = now.reshape(STACK, tok, HD)

    def passage_unit(q, step):
        at = pl.ds(step * group, group)
        keys = kvbuf[at, 0].reshape(group * keys_in, HD)
        values = kvbuf[at, 1].reshape(group * keys_in, HD)
        unit(q, keys, values)

    def suffix_unit(q):
        total = n_tp * tok
        shape = (STACK * tok, total)
        position = flip(rank, q, n_tp) * tok + lax.broadcasted_iota(jnp.int32, shape, 0) % tok
        unit(q, skbuf[...], svbuf[...], lax.broadcasted_iota(jnp.int32, shape, 1) > position)

    def await_step(step):
        @pl.loop(0, group)
        def _(g):
            kv_copy(step * group + g).wait_recv()

    near = n_tp // 2
    own[0].wait()
    own[1].wait()

    @pl.loop(1, group)
    def _(d):
        kv_copy(d).wait_recv()

    @pl.loop(0, near)
    def _(q):
        @pl.when(q > 0)
        def _():
            q_copy(q).wait_recv()

        passage_unit(q, 0)

    @pl.loop(1, steps - 1)
    def _(step):
        await_step(step)

        @pl.loop(0, near)
        def _(q):
            passage_unit(q, step)

    @pl.loop(near, n_tp)
    def _(q):
        q_copy(q).wait_recv()

        @pl.loop(0, steps - 1)
        def _(step):
            passage_unit(q, step)

    own[2].wait()
    own[3].wait()
    for d in range(1, n_tp):
        for copy in s_arrivals(d):
            copy.wait_recv()
    dk_ref[...] = skbuf[...]
    dv_ref[...] = svbuf[...]

    @pl.loop(0, n_tp)
    def _(q):
        suffix_unit(q)

    await_step(steps - 1)

    @pl.loop(0, n_tp)
    def _(turn):
        q = n_tp - 1 - turn
        passage_unit(q, steps - 1)
        for h in range(heads):
            whole = acc[q, h]
            obuf[q, :, h * HD:(h + 1) * HD] = (whole[:, :HD] / whole[:, HD:]).astype(jnp.bfloat16)

        @pl.when(q > 0)
        def _():
            c_copy(q).start()

    last = pltpu.make_async_copy(obuf.at[0], ctx_ref.at[:, columns(rank, width)], own_sem.at[0])
    last.start()

    @pl.loop(1, n_store)
    def _(d):
        kv_copy(d).wait_send()

    for d in range(1, n_tp):
        q_copy(d).wait_send()
        for copy in s_copies(d):
            copy.wait_send()
        c_copy(d).wait_send()
        c_arrival(d).wait_recv()
    last.wait()


def attend(queries, suffix_keys, suffix_values, send):
    n_store, n_tp = lax.axis_size("store"), lax.axis_size("tp")
    tok, total = queries.shape
    heads = total // n_tp // HD
    keys_in = send.shape[2]
    group = min(n_store, max(1, STEP_KEYS // keys_in))
    dtype = queries.dtype
    dma = pltpu.SemaphoreType.DMA
    any_spec = pl.BlockSpec(memory_space=pl.ANY)
    vmem = pl.BlockSpec(memory_space=pltpu.VMEM)
    suffix = jax.ShapeDtypeStruct((n_tp * tok, HD), dtype)
    return pl.pallas_call(
        functools.partial(attend_kernel, n_store, n_tp, group, heads),
        out_shape=(jax.ShapeDtypeStruct(queries.shape, dtype), suffix, suffix),
        in_specs=[any_spec] * 4,
        out_specs=(any_spec, vmem, vmem),
        scratch_shapes=[
            pltpu.VMEM((n_tp, tok, heads * HD), dtype),
            pltpu.VMEM((n_store, 2, keys_in, HD), dtype),
            pltpu.VMEM((n_tp * tok, HD), dtype),
            pltpu.VMEM((n_tp * tok, HD), dtype),
            pltpu.VMEM((n_tp, tok, heads * HD), dtype),
            pltpu.VMEM((n_tp, heads, tok, 2 * HD), jnp.float32),
            pltpu.VMEM((n_tp, heads, tok, HD), jnp.float32),
            dma((n_store,)), dma((n_store,)),
            dma((n_tp,)), dma((n_tp,)),
            dma((2, n_tp)), dma((2, n_tp)),
            dma((n_tp,)), dma((n_tp,)),
            dma((4,)),
        ],
        compiler_params=pltpu.CompilerParams(
            collective_id=0, has_side_effects=True, vmem_limit_bytes=48 * 1024 * 1024
        ),
        name="attend",
    )(queries, suffix_keys, suffix_values, send)


def body(queries, suffix_keys, suffix_values, passage_keys, passage_values, cites, passage_row, suffix_len):
    n_store, n_tp = lax.axis_size("store"), lax.axis_size("tp")
    me, rank = lax.axis_index("store"), lax.axis_index("tp")
    tok = queries.shape[1]
    length = suffix_len[me]
    partners = flip(me, jnp.arange(n_store, dtype=jnp.int32), n_store)
    rows = passage_row[cites[partners]]
    send = pick(rows, jnp.full((1,), rank, jnp.int32), passage_keys, passage_values)
    cite, part = send.shape[2], send.shape[3]
    context, keys, values = attend(
        queries[0], suffix_keys[0], suffix_values[0], send.reshape(n_store, 2, cite * part, HD)
    )
    positions = rank * tok + jnp.arange(tok, dtype=jnp.int32)
    context = jnp.where((positions < length)[:, None], context, jnp.zeros_like(context))
    live = (jnp.arange(n_tp * tok, dtype=jnp.int32) < length)[:, None]
    keys = jnp.where(live, keys, jnp.zeros_like(keys))
    values = jnp.where(live, values, jnp.zeros_like(values))
    return context[None], keys[None], values[None]


def solution(mesh):
    in_specs = (
        P("store", "tp", None),
        P("store", "tp", None),
        P("store", "tp", None),
        P(None, "store", None),
        P(None, "store", None),
        P(),
        P(),
        P(),
    )
    out_specs = (P("store", "tp", None), P("store", None, "tp"), P("store", None, "tp"))
    return jax.shard_map(body, mesh=mesh, in_specs=in_specs, out_specs=out_specs, check_vma=False)
```

time: 283 us -> 146 us (0.52)
  Pallas kernels: 0 us -> 136 us
  other arithmetic: 100 us -> 3.29 us
  matrix products: 56.1 us -> 0 us
  waiting for transfers between devices: 46.4 us -> 0 us
  local copies, waits for them, and re-layouts: 37.1 us -> 5.75 us
  blocking collectives: 31.3 us -> 0 us
  starting transfers between devices: 9.99 us -> 0 us
    pallas_call x0 -> x2, Pallas kernels: none -> 136 us  [the longest x1 70.7 us: attend(): pl.pallas_call(functools.partial(attend_kernel, n_store, n_tp, group, hea...]
    dot_general x8 -> x0, matrix products: 56.1 us -> none  [the longest x4 40.4 us: one_head(): jnp.einsum('rgk,kd->rgd', probs, value_g, preferred_element_type=jnp.floa...]
    sub x5 -> x0, other arithmetic: 53.8 us -> none  [the longest x4 53.7 us: one_head(): weights = jnp.exp(scores - peak)]
    all_to_all x2 -> x0, waiting for transfers between devices: 46.4 us -> none  [the longest x1 46.4 us: body(): lax.all_to_all(send_keys, 'store', split_axis=0, concat_axis=0, tiled=True)]
    transpose x2 -> x0, other arithmetic: 38.4 us -> none  [the longest x1 19.2 us: attend(): key_heads = keys.reshape(total, kv_count, HD).transpose(1, 0, 2)]
    all_gather x2 -> x0, blocking collectives: 31.3 us -> none  [the longest x1 16.4 us: body(): lax.all_gather(suffix_keys[0], 'tp', axis=0, tiled=True)]
    concatenate x4 -> x0, local copies, waits for them, and re-layouts: 14.5 us -> none  [the longest x2 7.29 us: body(): jnp.concatenate([got_values.reshape(-1, width), whole_values], axis=0)]
    all_to_all x2 -> x0, starting transfers between devices: 9.99 us -> none  [the longest x1 5.3 us: body(): lax.all_to_all(send_keys, 'store', split_axis=0, concat_axis=0, tiled=True)]
  transfers between devices with their start and end apart: 2 -> 0, of which waited for: 1 -> 0; matrix products, arithmetic and copies ran while one was open for 13% -> 0% of each run, Pallas kernels for 0% -> 0%
where the time goes in v1:
time: 146 us
  Pallas kernels  136 us (93%)
  local copies, waits for them, and re-layouts  5.75 us (4%)
  other arithmetic  3.29 us (2%)
    pallas_call x1, Pallas kernels, attend(): pl.pallas_call(functools.partial(attend_kernel, n_store, n_tp, group, hea...  70.7 us
    pallas_call x1, Pallas kernels, pick(): pl.pallas_call(functools.partial(pick_kernel, n, cite), out_shape=jax.Sha...  65.8 us

profile of v1, /device:TPU:0, one launch (start us, length us, event | category | flops | bytes accessed | tf_op | source)
XLA Modules:
  0.0 146.3 jit_solution(16948769520897344489)
XLA Ops:
  0.6 0.0 copy-start
  0.7 1.2 dynamic_slice.3
  1.9 0.7 add_compare_fusion
  2.6 0.7 iota_compare_fusion
  3.3 0.8 copy.14
  4.0 0.6 gather_fusion
  4.6 0.1 copy.15
  4.7 0.1 copy.16
  4.8 0.1 reshape.232
  4.8 0.0 copy-done
  4.9 0.7 gather_fusion.1
  5.5 0.7 reshape.231.rows_ref
  6.2 0.0 copy-start.2
  6.2 0.0 copy-start.3
  6.2 0.0 copy-start.4
  6.2 65.8 %pick.1 = bf16[8,2,2,256,128]{4,3,2,1,0:T(8,128)(2,1)} custom-call(s32[8,2]{1,0:T(8,128)} %reshape.231.rows_ref, s32[1]{0:T(128)} %bitcast.6.rank_ref, bf16[8,256,512]{2,1,0:T(8,128)(2,1)} %pk_ref.1, bf16[8,256,512]{2,1,0:T(8,128)(2,1)} %pv_ref.1), custom_call_target="tpu_custom_call" | custom-call | tf_op jit(solution)/shard_map/pick/pallas_call | solution.py:54
  72.0 0.0 copy-done.2
  72.0 0.0 copy-done.3
  72.0 0.0 copy-done.4
  72.0 0.0 copy-start.1
  72.0 1.6 %copy-done.1 = bf16[8,2,2,256,128]{4,3,2,1,0:T(8,128)(2,1)S(1)} copy-done((bf16[8,2,2,256,128]{4,3,2,1,0:T(8,128)(2,1)S(1)}, bf16[8,2,2,256,128]{4,3,2,1,0:T(8,128)(2,1)}, u32[]{:S(2)}) %copy-start.1) | copy-done | bytes 2097176
  73.6 70.7 %attend.1 = (bf16[128,4096]{1,0:T(8,128)(2,1)S(1)}, bf16[512,128]{1,0:T(8,128)(2,1)S(1)}, bf16[512,128]{1,0:T(8,128)(2,1)S(1)}) custom-call(bf16[128,4096]{1,0:T(8,128)(2,1)S(1)} %bitcast.19, bf16[128,512]{1,0:T(8,128)(2,1)S(1)} %bitcast.20, bf16[128,512]{1,0:T(8,128)(2,1)S(1)} %bitcast.21, bf16[8,2,512,128]{3,2,1,0:T(8,128)(2,1)S(1)} %bitcast.18), custom_call_target="tpu_custom_call" | custom-call | tf_op jit(solution)/shard_map/attend/pallas_call | solution.py:301
  144.3 1.1 select_bitcast_fusion
  145.4 0.8 select_bitcast_fusion.1
  (4 shorter events, 0.0 us)
Async XLA Ops:
  0.6 4.2 %copy-start = (s32[8]{0:T(128)S(1)}, s32[8]{0:T(128)}, u32[]{:S(2)}) copy-start(s32[8]{0:T(128)} %param.14) | copy-start | bytes 100
  6.2 65.8 %copy-start.2 = (bf16[1,128,4096]{2,1,0:T(8,128)(2,1)S(1)}, bf16[1,128,4096]{2,1,0:T(8,128)(2,1)}, u32[]{:S(2)}) copy-start(bf16[1,128,4096]{2,1,0:T(8,128)(2,1)} %param.8) | copy-start | bytes 3145732
  6.2 65.8 %copy-start.3 = (bf16[1,128,512]{2,1,0:T(8,128)(2,1)S(1)}, bf16[1,128,512]{2,1,0:T(8,128)(2,1)}, u32[]{:S(2)}) copy-start(bf16[1,128,512]{2,1,0:T(8,128)(2,1)} %param.9) | copy-start | bytes 393220
  6.2 65.8 %copy-start.4 = (bf16[1,128,512]{2,1,0:T(8,128)(2,1)S(1)}, bf16[1,128,512]{2,1,0:T(8,128)(2,1)}, u32[]{:S(2)}) copy-start(bf16[1,128,512]{2,1,0:T(8,128)(2,1)} %param.10) | copy-start | bytes 393220
  72.0 1.6 %copy-start.1 = (bf16[8,2,2,256,128]{4,3,2,1,0:T(8,128)(2,1)S(1)}, bf16[8,2,2,256,128]{4,3,2,1,0:T(8,128)(2,1)}, u32[]{:S(2)}) copy-start(bf16[8,2,2,256,128]{4,3,2,1,0:T(8,128)(2,1)} %pick.1) | copy-start | bytes 6291460

commit v2 on v1

--- a/solution.py
+++ b/solution.py
@@ -60,7 +60,7 @@
             pl.BlockSpec(memory_space=pl.ANY),
             pl.BlockSpec(memory_space=pl.ANY),
         ],
-        out_specs=pl.BlockSpec(memory_space=pl.ANY),
+        out_specs=pl.BlockSpec(memory_space=pltpu.VMEM),
         scratch_shapes=[pltpu.SemaphoreType.DMA((n, cite, 2))],
         name="pick",
     )(rows, rank, passage_keys, passage_values)
@@ -69,7 +69,7 @@
 def attend_kernel(
     n_store, n_tp, group, heads,
     q_ref, sk_ref, sv_ref, send_ref, ctx_ref, dk_ref, dv_ref,
-    qbuf, kvbuf, skbuf, svbuf, obuf, acc, peak,
+    qbuf, qwide, kvbuf, skbuf, svbuf, obuf, acc, peak,
     kv_send, kv_recv, q_send, q_recv, s_send, s_recv, c_send, c_recv, own_sem,
 ):
     me = lax.axis_index("store")
@@ -155,7 +155,7 @@
         pl.semaphore_signal(barrier, inc=1, device_id=(me, flip(rank, d, n_tp)), device_id_type=MESH)
     pl.semaphore_wait(barrier, n_store - 1 + n_tp - 1)
 
-    for d in range(1, n_tp):
+    for d in [n_tp - 1, *range(1, n_tp - 1)]:
         q_copy(d).start()
 
     @pl.loop(1, n_store)
@@ -172,22 +172,20 @@
     def unit(q, keys, values, hidden=None):
         count = keys.shape[0]
         wide = jnp.concatenate([values, jnp.ones_like(values)], axis=1)
+        twice = jnp.concatenate([keys, keys], axis=1)
         for first in range(0, heads, STACK):
-            stacked = jnp.concatenate(
-                [qbuf[q, :, h * HD:(h + 1) * HD] for h in range(first, first + STACK)], axis=0
-            )
+            stacked = qwide[q, first:first + STACK].reshape(STACK * tok, 2 * HD)
             scores = lax.dot_general(
-                stacked, keys, (((1,), (1,)), ((), ())), preferred_element_type=jnp.float32
+                stacked, twice, (((1,), (1,)), ((), ())), preferred_element_type=jnp.float32
             )
             if hidden is not None:
                 scores = jnp.where(hidden, -1e30, scores)
             rows = STACK * tok
             before = peak[q, first:first + STACK].reshape(rows, HD)
             now = jnp.maximum(before, jnp.max(scores, axis=1, keepdims=True))
-            decay = jnp.exp2((before - now) * FACTOR)
-            base = now * FACTOR
+            decay = jnp.exp2(before - now)
             weights = jnp.exp2(
-                scores * FACTOR - jnp.concatenate([base] * (count // HD), axis=1)
+                scores - jnp.concatenate([now] * (count // HD), axis=1)
             ).astype(jnp.bfloat16)
             part = jnp.dot(weights, wide, preferred_element_type=jnp.float32)
             held = acc[q, first:first + STACK].reshape(rows, 2 * HD)
@@ -196,6 +194,13 @@
             ).reshape(STACK, tok, 2 * HD)
             peak[q, first:first + STACK] = now.reshape(STACK, tok, HD)
 
+    def prepare(q):
+        for h in range(heads):
+            scaled = qbuf[q, :, h * HD:(h + 1) * HD].astype(jnp.float32) * FACTOR
+            high = scaled.astype(jnp.bfloat16)
+            low = (scaled - high.astype(jnp.float32)).astype(jnp.bfloat16)
+            qwide[q, h] = jnp.concatenate([high, low], axis=1)
+
     def passage_unit(q, step):
         at = pl.ds(step * group, group)
         keys = kvbuf[at, 0].reshape(group * keys_in, HD)
@@ -213,7 +218,7 @@
         def _(g):
             kv_copy(step * group + g).wait_recv()
 
-    near = n_tp // 2
+    far = n_tp - 1
     own[0].wait()
     own[1].wait()
 
@@ -221,47 +226,55 @@
     def _(d):
         kv_copy(d).wait_recv()
 
-    @pl.loop(0, near)
-    def _(q):
-        @pl.when(q > 0)
+    @pl.loop(0, 2)
+    def _(j):
+        q = j * far
+
+        @pl.when(j > 0)
         def _():
             q_copy(q).wait_recv()
 
+        prepare(q)
         passage_unit(q, 0)
 
     @pl.loop(1, steps - 1)
     def _(step):
         await_step(step)
 
-        @pl.loop(0, near)
-        def _(q):
-            passage_unit(q, step)
-
-    @pl.loop(near, n_tp)
-    def _(q):
+        @pl.loop(0, 2)
+        def _(j):
+            passage_unit(j * far, step)
+
+    def catch_up(q):
         q_copy(q).wait_recv()
+        prepare(q)
 
         @pl.loop(0, steps - 1)
         def _(step):
             passage_unit(q, step)
 
-    own[2].wait()
-    own[3].wait()
-    for d in range(1, n_tp):
-        for copy in s_arrivals(d):
-            copy.wait_recv()
-    dk_ref[...] = skbuf[...]
-    dv_ref[...] = svbuf[...]
-
-    @pl.loop(0, n_tp)
-    def _(q):
-        suffix_unit(q)
-
-    await_step(steps - 1)
+    catch_up(1)
 
     @pl.loop(0, n_tp)
     def _(turn):
         q = n_tp - 1 - turn
+
+        @pl.when((q > 1) & (q < far))
+        def _():
+            catch_up(q)
+
+        @pl.when(turn == 0)
+        def _():
+            own[2].wait()
+            own[3].wait()
+            for d in range(1, n_tp):
+                for copy in s_arrivals(d):
+                    copy.wait_recv()
+            dk_ref[...] = skbuf[...]
+            dv_ref[...] = svbuf[...]
+            await_step(steps - 1)
+
+        suffix_unit(q)
         passage_unit(q, steps - 1)
         for h in range(heads):
             whole = acc[q, h]
@@ -305,6 +318,7 @@
         out_specs=(any_spec, vmem, vmem),
         scratch_shapes=[
             pltpu.VMEM((n_tp, tok, heads * HD), dtype),
+            pltpu.VMEM((n_tp, heads, tok, 2 * HD), dtype),
             pltpu.VMEM((n_store, 2, keys_in, HD), dtype),
             pltpu.VMEM((n_tp * tok, HD), dtype),
             pltpu.VMEM((n_tp * tok, HD), dtype),

time: 146 us -> 76.1 us (0.52)
  Pallas kernels: 136 us -> 65.9 us
    pallas_call x1, Pallas kernels: 65.8 us -> 4.13 us  [pick(): pl.pallas_call(functools.partial(pick_kernel, n, cite), out_shape=jax.Sha...]
    pallas_call x1, Pallas kernels: 70.7 us -> 61.8 us  [attend(): pl.pallas_call(functools.partial(attend_kernel, n_store, n_tp, group, hea...]
where the time goes in v2:
time: 76.1 us; the launch traced here: 75.7 us
  Pallas kernels  65.9 us (87%)
  local copies, waits for them, and re-layouts  5.75 us (8%)
  other arithmetic  3.29 us (4%)
    pallas_call x1, Pallas kernels, attend(): pl.pallas_call(functools.partial(attend_kernel, n_store, n_tp, group, hea...  61.8 us
    pallas_call x1, Pallas kernels, pick(): pl.pallas_call(functools.partial(pick_kernel, n, cite), out_shape=jax.Sha...  4.13 us
    unnamed x11, local copies, waits for them, and re-layouts  2.36 us
    gather x4, local copies, waits for them, and re-layouts, body(): rows = passage_row[cites[partners]]  1.98 us
    broadcast_in_dim x2, other arithmetic, body(): return (context[None], keys[None], values[None])  1.95 us

profile of v2, /device:TPU:0, one launch (start us, length us, event | category | flops | bytes accessed | tf_op | source)
XLA Modules:
  0.0 75.7 jit_solution(13003391260784212547)
XLA Ops:
  0.6 0.0 copy-start
  0.7 1.2 %dynamic_slice.3 = s32[1]{0:T(128)} dynamic-slice(s32[8]{0:T(128)} %param.15, s32[]{:T(128)S(6)} %select_n.102), dynamic_slice_sizes={1} | dynamic-slice | bytes 12 | tf_op jit(solution)/shard_map/dynamic_slice | solution.py:345
  1.9 0.7 add_compare_fusion
  2.6 0.7 iota_compare_fusion
  3.3 0.8 copy.14
  4.0 0.6 gather_fusion
  4.6 0.1 copy.15
  4.7 0.1 copy.16
  4.8 0.1 reshape.232
  4.8 0.0 copy-done
  4.9 0.7 gather_fusion.1
  5.5 0.7 reshape.231.rows_ref
  6.2 0.0 copy-start.2
  6.2 0.0 copy-start.3
  6.2 0.0 copy-start.4
  6.2 4.1 %pick.1 = bf16[8,2,2,256,128]{4,3,2,1,0:T(8,128)(2,1)} custom-call(s32[8,2]{1,0:T(8,128)} %reshape.231.rows_ref, s32[1]{0:T(128)} %bitcast.6.rank_ref, bf16[8,256,512]{2,1,0:T(8,128)(2,1)} %pk_ref.1, bf16[8,256,512]{2,1,0:T(8,128)(2,1)} %pv_ref.1), custom_call_target="tpu_custom_call" | custom-call | tf_op jit(solution)/shard_map/pick/pallas_call | solution.py:54
  10.3 0.0 copy-done.2
  10.4 0.0 copy-done.3
  10.4 0.0 copy-done.4
  10.4 0.0 copy-start.1
  10.4 1.6 %copy-done.1 = bf16[8,2,2,256,128]{4,3,2,1,0:T(8,128)(2,1)S(1)} copy-done((bf16[8,2,2,256,128]{4,3,2,1,0:T(8,128)(2,1)S(1)}, bf16[8,2,2,256,128]{4,3,2,1,0:T(8,128)(2,1)}, u32[]{:S(2)}) %copy-start.1) | copy-done | bytes 2097176
  12.0 61.8 %attend.1 = (bf16[128,4096]{1,0:T(8,128)(2,1)S(1)}, bf16[512,128]{1,0:T(8,128)(2,1)S(1)}, bf16[512,128]{1,0:T(8,128)(2,1)S(1)}) custom-call(bf16[128,4096]{1,0:T(8,128)(2,1)S(1)} %bitcast.19, bf16[128,512]{1,0:T(8,128)(2,1)S(1)} %bitcast.20, bf16[128,512]{1,0:T(8,128)(2,1)S(1)} %bitcast.21, bf16[8,2,512,128]{3,2,1,0:T(8,128)(2,1)S(1)} %bitcast.18), custom_call_target="tpu_custom_call" | custom-call | tf_op jit(solution)/shard_map/attend/pallas_call | solution.py:314
  73.8 1.1 %select_bitcast_fusion = bf16[1,128,4096]{2,1,0:T(8,128)(2,1)} fusion(bf16[128,4096]{1,0:T(8,128)(2,1)S(1)} %get-tuple-element.6, pred[128]{0:T(512)(128)(4,1)S(1)} %add_compare_fusion), kind=kLoop, calls=%fused_computation.2 | loop fusion | flops 524288 | bytes 2097280 | tf_op jit(solution)/shard_map/broadcast_in_dim | solution.py:358
  74.9 0.8 %select_bitcast_fusion.1 = (bf16[1,512,128]{2,1,0:T(8,128)(2,1)}, bf16[1,512,128]{2,1,0:T(8,128)(2,1)}) fusion(bf16[512,128]{1,0:T(8,128)(2,1)S(1)} %get-tuple-element.8, pred[512]{0:T(512)(128)(4,1)S(1)} %iota_compare_fusion, bf16[512,128]{1,0:T(8,128)(2,1)S(1)} %get-tuple-element.7), kind=kLoop, calls=%fused_computation.3 | loop fusion | flops 131072 | bytes 524800 | tf_op jit(solution)/shard_map/broadcast_in_dim | solution.py:358
  (4 shorter events, 0.0 us)
Async XLA Ops:
  0.6 4.2 %copy-start = (s32[8]{0:T(128)S(1)}, s32[8]{0:T(128)}, u32[]{:S(2)}) copy-start(s32[8]{0:T(128)} %param.14) | copy-start | bytes 100
  6.2 4.1 %copy-start.2 = (bf16[1,128,4096]{2,1,0:T(8,128)(2,1)S(1)}, bf16[1,128,4096]{2,1,0:T(8,128)(2,1)}, u32[]{:S(2)}) copy-start(bf16[1,128,4096]{2,1,0:T(8,128)(2,1)} %param.8) | copy-start | bytes 3145732
  6.2 4.2 %copy-start.3 = (bf16[1,128,512]{2,1,0:T(8,128)(2,1)S(1)}, bf16[1,128,512]{2,1,0:T(8,128)(2,1)}, u32[]{:S(2)}) copy-start(bf16[1,128,512]{2,1,0:T(8,128)(2,1)} %param.9) | copy-start | bytes 393220
  6.2 4.2 %copy-start.4 = (bf16[1,128,512]{2,1,0:T(8,128)(2,1)S(1)}, bf16[1,128,512]{2,1,0:T(8,128)(2,1)}, u32[]{:S(2)}) copy-start(bf16[1,128,512]{2,1,0:T(8,128)(2,1)} %param.10) | copy-start | bytes 393220
  10.4 1.6 %copy-start.1 = (bf16[8,2,2,256,128]{4,3,2,1,0:T(8,128)(2,1)S(1)}, bf16[8,2,2,256,128]{4,3,2,1,0:T(8,128)(2,1)}, u32[]{:S(2)}) copy-start(bf16[8,2,2,256,128]{4,3,2,1,0:T(8,128)(2,1)} %pick.1) | copy-start | bytes 6291460
